TPU v7x, 32 devices: a whole 2x2x4 slice. The times are simulated.
32 devices in a mesh: trk: 8 (over z, x), cam: 4 (over y, core).
Axes of the slice: x: 2, y: 2, z: 4, core: 2. Of those that a mesh axis runs over, the one named last changes fastest.
Arguments:
- residuals: float32 [2, 24576], P(None, ('trk', 'cam')), may hold values from -6 to 6
- camera_jac: float32 [18, 24576], P(None, ('trk', 'cam')), may hold values from -9 to 9
- point_jac: float32 [6, 24576], P(None, ('trk', 'cam')), may hold values from -6 to 6
- obs_index: int32 [3, 24576], P(None, ('trk', 'cam')), may hold values from 0 to 767, as said below
- damping: float32 [2048], P('trk'), may hold values from 0.5 to 4
Outputs:
- elimination_tiles: float32 [8, 4, 7, 20736], P('trk', 'cam')
Inputs may be any that keep to these rules, and one draw needn't show every extreme that they name: For each c and e, the values obs_index[0, n] of the rows n = ((t * 4 + c) * 8 + e) * 96 + q over all t and q are a permutation of 0 to 767. The camera obs_index[1, n] of such a row lies in a block (camera // 16) among 2 * e to 2 * e + 7, taken modulo 16. obs_index[2, n] is 1 for a live observation and 0 for a padded slot.
All inputs are finite; a program needn't handle non-finite values.
Results may differ from a plain program's by a relative error of at most 0.0003.
Values sent between devices are 32-bit elements; how exact they have to be, the bound alone decides.
A program may use at most 64 MiB of HBM per device.

v0:
```python
import functools

import jax
import jax.numpy as jnp
import numpy as np
from jax import lax
from jax.experimental import pallas as pl
from jax.experimental.pallas import tpu as pltpu
from jax.sharding import PartitionSpec as P

CAMERAS_PER_BLK = 16
TS = 144
HOPS = 3
OWNERS = HOPS + 1
TILES = 2 * HOPS + 1
KC = 3
TRACKS = 256
SLOTS = 12
LANES = 128
MSG = 152
DIRECT_DEVICES = 8
MESH = pl.DeviceIdType.MESH


def split(x):
    high = x.astype(jnp.bfloat16)
    low = (x - high.astype(jnp.float32)).astype(jnp.bfloat16)
    return high, low


def scaled_rows(residuals, camera_jac, point_jac, index):
    first, second = residuals[0:1], residuals[1:2]
    magnitude = jnp.sqrt(first * first + second * second)
    weight = index[2:3].astype(jnp.float32) / jnp.maximum(magnitude, 1.0)
    root = jnp.sqrt(weight)
    return (
        camera_jac * root,
        point_jac * root,
        index[1:2].astype(jnp.float32),
        index[0:1].astype(jnp.float32),
    )


def exchange_body(direct, n, *refs):
    if direct:
        res_ref, cam_ref, pnt_ref, idx_ref, damp_ref, got_ref = refs[:6]
        rows_ref, send_ref, recv_ref, ssem1, rsem1, ssem2, rsem2, ssem3, rsem3 = refs[6:]
    else:
        rows_ref, damp_ref, got_ref = refs[:3]
        ssem2, rsem2, ssem3, rsem3 = refs[3:]
    me = lax.axis_index("trk")
    col = lax.axis_index("cam")
    core = col + 1 - 2 * lax.rem(col, 2)
    side = lax.rem(col + 2, 4)

    def ahead(by):
        return lax.rem(me + by, n)

    barrier = pltpu.get_barrier_semaphore()
    steps = range(1, n) if direct else (1, 2, 3, n - 3, n - 2, n - 1)
    for by in steps:
        pl.semaphore_signal(barrier, inc=1, device_id=(ahead(by), col), device_id_type=MESH)
    for other in (core, side):
        pl.semaphore_signal(barrier, inc=1, device_id=(me, other), device_id_type=MESH)

    if direct:
        width = rows_ref.shape[1] // n
        cj, pj, camera, position = scaled_rows(res_ref[...], cam_ref[...], pnt_ref[...], idx_ref[...])
        rows_ref[0:18] = cj
        rows_ref[18:24] = pj
        rows_ref[24:25] = camera
        rows_ref[25:26] = position
        rows_ref[26:32] = jnp.zeros((6, rows_ref.shape[1]), jnp.float32)
        rows = rows_ref[...]
        lane = lax.broadcasted_iota(jnp.int32, (32, LANES), 1)
        row = lax.broadcasted_iota(jnp.int32, (32, LANES), 0)
        fill = jnp.where(row == 25, -1.0, 0.0)
        for e in range(n):
            start = e * width
            piece = rows if start == 0 else pltpu.roll(rows, rows.shape[1] - start, 1)
            send_ref[e] = jnp.where(lane < width, piece[:, :LANES], fill)
    pl.semaphore_wait(barrier, len(steps) + 2)

    if direct:
        copies = []
        for by in range(1, n):
            copy = pltpu.make_async_remote_copy(
                src_ref=send_ref.at[ahead(by)],
                dst_ref=recv_ref.at[by],
                send_sem=ssem1.at[by],
                recv_sem=rsem1.at[by],
                device_id=(ahead(by), col),
                device_id_type=MESH,
            )
            copy.start()
            copies.append(copy)
        recv_ref[0] = send_ref[me]
        for copy in copies:
            copy.wait()
        chunks = [recv_ref[k] for k in range(n)]
    else:
        chunks = [rows_ref[:, k * LANES : (k + 1) * LANES] for k in range(rows_ref.shape[1] // LANES)]

    slot = lax.broadcasted_iota(jnp.int32, (KC * TRACKS, LANES), 0).astype(jnp.float32)
    places, values = [], []
    for chunk in chunks:
        places.append(jnp.where(slot == chunk[25:26], 1.0, 0.0).astype(jnp.bfloat16))
        high, low = split(chunk)
        values.append(jnp.concatenate([high, low], axis=0))
    placed = lax.dot_general(
        jnp.concatenate(values, axis=1),
        jnp.concatenate(places, axis=1),
        (((1,), (1,)), ((), ())),
        preferred_element_type=jnp.float32,
    )
    placed = placed[:32] + placed[32:]
    tiles = KC * TRACKS // LANES
    for r in range(3):
        for l in range(tiles):
            at = (r * tiles + l) * 8
            got_ref[0, 0, at : at + 8] = placed[8 * r : 8 * r + 8, l * LANES : (l + 1) * LANES]
    for l in range(tiles):
        got_ref[0, 0, 144 + l : 145 + l] = placed[24:25, l * LANES : (l + 1) * LANES]
    for l in range(2):
        got_ref[0, 0, 150 + l : 151 + l] = damp_ref[:, l * LANES : (l + 1) * LANES]

    def send(src, dst, ssem, rsem, device):
        copy = pltpu.make_async_remote_copy(
            src_ref=src, dst_ref=dst, send_sem=ssem, recv_sem=rsem, device_id=device, device_id_type=MESH
        )
        copy.start()
        return copy

    along = [None]
    for h in range(1, OWNERS):
        along.append(
            send(got_ref.at[0, 0], got_ref.at[h, 0], ssem2.at[h], rsem2.at[h], (ahead(h), col))
        )
    sides, cores, passed = [], [], []
    for h in range(OWNERS):
        if h:
            along[h].wait_recv()
        sides.append(
            send(got_ref.at[h, 0], got_ref.at[h, 2], ssem3.at[h, 2], rsem3.at[h, 2], (me, side))
        )
        cores.append(
            send(got_ref.at[h, 0], got_ref.at[h, 1], ssem3.at[h, 1], rsem3.at[h, 1], (me, core))
        )
    for h in range(OWNERS):
        sides[h].wait_recv()
        passed.append(
            send(got_ref.at[h, 2], got_ref.at[h, 3], ssem3.at[h, 3], rsem3.at[h, 3], (me, core))
        )
    for h in range(OWNERS):
        cores[h].wait_recv()
        passed[h].wait_recv()
    for copy in along[1:] + sides + cores + passed:
        copy.wait_send()


def exchange(n, direct, damping, *arrays):
    vmem = pl.BlockSpec(memory_space=pltpu.VMEM)
    dma = pltpu.SemaphoreType.DMA
    scratch = []
    if direct:
        scratch += [
            pltpu.VMEM((32, arrays[0].shape[1]), jnp.float32),
            pltpu.VMEM((n, 32, LANES), jnp.float32),
            pltpu.VMEM((n, 32, LANES), jnp.float32),
            dma((n,)),
            dma((n,)),
        ]
    scratch += [dma((OWNERS,)), dma((OWNERS,)), dma((OWNERS, 4)), dma((OWNERS, 4))]
    return pl.pallas_call(
        functools.partial(exchange_body, direct, n),
        out_shape=jax.ShapeDtypeStruct((OWNERS, 4, MSG, LANES), jnp.float32),
        in_specs=[vmem] * (len(arrays) + 1),
        out_specs=vmem,
        scratch_shapes=scratch,
        compiler_params=pltpu.CompilerParams(
            collective_id=0, has_side_effects=True, vmem_limit_bytes=32 * 2**20
        ),
        name="exchange",
    )(*arrays, damping.reshape(1, TRACKS))


def tiles_body(n, got_ref, repeat_ref, group_ref, out_ref, rep, coup, view, left, right, acc_a, acc_b):
    me = lax.axis_index("trk")
    col = lax.axis_index("cam")
    cameras = 2 * n * CAMERAS_PER_BLK
    left_parity = col // 2
    right_parity = lax.rem(col, 2)
    acc_a[...] = jnp.zeros_like(acc_a)
    acc_b[...] = jnp.zeros_like(acc_b)

    def jac_tile(h, part, r, l):
        return got_ref[h, part, (r * 6 + l) * 8 : (r * 6 + l) * 8 + 8]

    def per_slab(h, _):
        slab = lax.rem(me + n - h, n)

        def per_part(part, sums):
            sums = list(sums)
            blocks = [
                jnp.concatenate([jac_tile(h, part, r, l) for r in range(3)], axis=0) for l in range(6)
            ]
            values = jnp.concatenate(blocks, axis=1)
            high, low = split(values)
            rep[...] = lax.dot_general(
                repeat_ref[...],
                jnp.concatenate([high, low], axis=0),
                (((1,), (0,)), ((), ())),
                preferred_element_type=jnp.float32,
            )
            for l in range(6):
                j, half = l // 2, l % 2
                where = part * 6 + l
                seen = got_ref[h, part, 144 + l : 145 + l].astype(jnp.int32) - 2 * CAMERAS_PER_BLK * slab
                view[where] = jnp.broadcast_to(jnp.where(seen < 0, seen + cameras, seen), (8, LANES))
                tile = blocks[l][16:24]
                first = [tile[2 + k : 3 + k] for k in range(3)]
                second = [tile[5 + k : 6 + k] for k in range(3)]
                one = rep[0:72, l * LANES : (l + 1) * LANES]
                two = rep[72:144, l * LANES : (l + 1) * LANES]
                for k in range(3):
                    coup[where, k] = one * first[k] + two * second[k]
                at = 6 * half
                for k, m in ((0, 0), (0, 1), (0, 2), (1, 1), (1, 2), (2, 2)):
                    sums[at] = sums[at] + first[k] * first[m] + second[k] * second[m]
                    at += 1
            return tuple(sums)

        sums = lax.fori_loop(0, 4, per_part, tuple(jnp.zeros((1, LANES), jnp.float32) for _ in range(12)))

        inverse = []
        for half in range(2):
            a, b, c, d, e, f = sums[6 * half : 6 * half + 6]
            damp = got_ref[h, 0, 150 + half : 151 + half]
            a, d, f = a + damp, d + damp, f + damp
            cof = [d * f - e * e, c * e - b * f, b * e - c * d, a * f - c * c, b * c - a * e, a * d - b * b]
            det = a * cof[0] + b * cof[1] + c * cof[2]
            cof = [x / det for x in cof]
            inverse.append([[cof[i] for i in order] for order in ((0, 1, 2), (1, 3, 4), (2, 4, 5))])

        group = group_ref[...]

        def gather(first_camera, half):
            halves = []
            for g in range(2):
                base = first_camera + 8 * g
                total = [None] * 3
                for s in range(SLOTS):
                    where = 2 * s + half
                    target = view[where] - base
                    mask = group == jnp.concatenate([target] * 9, axis=0)
                    for k in range(3):
                        term = jnp.where(mask, coup[where, k], 0.0)
                        total[k] = term if s == 0 else total[k] + term
                halves.append(total)
            return [jnp.concatenate([halves[0][k], halves[1][k]], axis=0) for k in range(3)]

        def store(ref, at, k, half, value):
            high, low = split(value)
            lanes = slice(k * TRACKS + half * LANES, k * TRACKS + (half + 1) * LANES)
            if at is None:
                ref[0, :, lanes] = high
                ref[1, :, lanes] = low
            else:
                ref[0, at, :, lanes] = high
                ref[1, at, :, lanes] = low

        for half in range(2):
            panel = gather(CAMERAS_PER_BLK * (2 * h + left_parity), half)
            inv = inverse[half]
            for k in range(3):
                solved = panel[0] * inv[0][k] + panel[1] * inv[1][k] + panel[2] * inv[2][k]
                store(left, None, k, half, solved)

        def per_block(m, _):
            for half in range(2):
                panel = gather(CAMERAS_PER_BLK * (2 * m + right_parity), half)
                for k in range(3):
                    store(right, m, k, half, panel[k])
            return 0

        lax.fori_loop(0, OWNERS, per_block, 0)

        def per_tile(m, _):
            def product(i, j):
                return lax.dot_general(
                    left[i], right[j, m], (((1,), (1,)), ((), ())), preferred_element_type=jnp.float32
                )

            tile = product(0, 0) + (product(0, 1) + product(1, 0))
            at = pl.multiple_of((HOPS - h + m) * TS, 8)
            acc_a[pl.ds(at, TS), :] += tile[:, :LANES]
            acc_b[pl.ds(at, TS), 0 : TS - LANES] += tile[:, LANES:]
            return 0

        lax.fori_loop(0, OWNERS, per_tile, 0)
        return 0

    lax.fori_loop(0, OWNERS, per_slab, 0)

    lane = lax.broadcasted_iota(jnp.int32, (TILES, LANES), 1)

    def flatten(q, _):
        main, tail = [], []
        for i in range(8):
            rows = pl.ds(q * 8 + i, TILES, stride=TS)
            a, b = acc_a[rows, :], acc_b[rows, :]
            main.append(a if i == 0 else pltpu.roll(a, 16 * i, 1))
            tail.append(b if i == 0 else pltpu.roll(b, 16 * i, 1))
        for t in range(9):
            if t == 0:
                value = main[0]
            else:
                value = jnp.where(lane >= 16 * (t - 1), tail[t - 1], main[t - 1])
                if t < 8:
                    value = jnp.where(lane >= 16 * t, main[t], value)
            out_ref[0, 0, :, pl.ds(pl.multiple_of(q * 9 * LANES, LANES) + t * LANES, LANES)] = value
        return 0

    lax.fori_loop(0, TS // 8, flatten, 0)


def tiles(n, got):
    rows = np.arange(TS)
    repeat = np.zeros((TS, 24), np.float32)
    repeat[rows, np.where(rows < 72, rows % 9, 9 + rows % 9)] = 1.0
    repeat = jnp.asarray(np.concatenate([repeat, repeat], axis=1), jnp.bfloat16)
    group = jnp.asarray(np.broadcast_to((np.arange(72) // 9)[:, None], (72, LANES)).astype(np.int32))
    vmem = pl.BlockSpec(memory_space=pltpu.VMEM)
    return pl.pallas_call(
        functools.partial(tiles_body, n),
        out_shape=jax.ShapeDtypeStruct((1, 1, TILES, TS * TS), jnp.float32),
        in_specs=[vmem] * 3,
        out_specs=vmem,
        scratch_shapes=[
            pltpu.VMEM((TS, KC * TRACKS), jnp.float32),
            pltpu.VMEM((2 * SLOTS, 3, 72, LANES), jnp.float32),
            pltpu.VMEM((2 * SLOTS, 8, LANES), jnp.int32),
            pltpu.VMEM((2, TS, 3 * TRACKS), jnp.bfloat16),
            pltpu.VMEM((2, OWNERS, TS, 3 * TRACKS), jnp.bfloat16),
            pltpu.VMEM((TILES * TS, LANES), jnp.float32),
            pltpu.VMEM((TILES * TS, LANES), jnp.float32),
        ],
        compiler_params=pltpu.CompilerParams(vmem_limit_bytes=48 * 2**20),
        name="tiles",
    )(got, repeat, group)


def body(n, residuals, camera_jac, point_jac, obs_index, damping):
    direct = n <= DIRECT_DEVICES
    if direct:
        got = exchange(n, True, damping, residuals, camera_jac, point_jac, obs_index)
    else:
        rows = jnp.concatenate(scaled_rows(residuals, camera_jac, point_jac, obs_index), axis=0)
        rows = lax.all_to_all(rows, "trk", split_axis=1, concat_axis=1, tiled=True)
        got = exchange(n, False, damping, jnp.pad(rows, ((0, 6), (0, 0))))
    return tiles(n, got)


def solution(mesh):
    by_row = P(None, ("trk", "cam"))
    return jax.shard_map(
        functools.partial(body, mesh.shape["trk"]),
        mesh=mesh,
        in_specs=(by_row, by_row, by_row, by_row, P("trk")),
        out_specs=P("trk", "cam", None, None),
        check_vma=False,
    )
```

profile of v0, /device:TPU:0, one launch (start us, length us, event | category | flops | bytes accessed | tf_op | source)
XLA Modules:
  0.0 52.0 jit_solution(15990670684927717306)
XLA Ops:
  0.0 0.0 copy-start
  0.0 0.9 %copy-done = f32[18,768]{1,0:T(8,128)S(1)} copy-done((f32[18,768]{1,0:T(8,128)S(1)}, f32[18,768]{1,0:T(8,128)}, u32[]{:S(2)}) %copy-start) | copy-done | bytes 55320
  0.9 0.0 copy-start.3
  0.9 0.7 %copy-done.3 = f32[6,768]{1,0:T(8,128)S(1)} copy-done((f32[6,768]{1,0:T(8,128)S(1)}, f32[6,768]{1,0:T(8,128)}, u32[]{:S(2)}) %copy-start.3) | copy-done | bytes 18456
  1.6 0.0 copy-start.4
  1.6 0.7 %copy-done.4 = s32[3,768]{1,0:T(4,128)S(1)} copy-done((s32[3,768]{1,0:T(4,128)S(1)}, s32[3,768]{1,0:T(4,128)}, u32[]{:S(2)}) %copy-start.4) | copy-done | bytes 9240
  2.3 0.0 copy-start.5
  2.3 0.7 %copy-done.5 = f32[2,768]{1,0:T(2,128)S(1)} copy-done((f32[2,768]{1,0:T(2,128)S(1)}, f32[2,768]{1,0:T(2,128)}, u32[]{:S(2)}) %copy-start.5) | copy-done | bytes 6168
  3.0 0.0 copy-start.6
  3.0 0.7 %copy-done.6 = f32[256]{0:T(256)S(1)} copy-done((f32[256]{0:T(256)S(1)}, f32[256]{0:T(256)}, u32[]{:S(2)}) %copy-start.6) | copy-done | bytes 1048
  3.7 0.0 copy-start.1
  3.7 0.0 copy-start.2
  3.7 24.7 %exchange.1.got_ref = f32[4,4,152,128]{3,2,1,0:T(8,128)S(1)} custom-call(f32[2,768]{1,0:T(2,128)S(1)} %copy-done.5, f32[18,768]{1,0:T(8,128)S(1)} %copy-done, f32[6,768]{1,0:T(8,128)S(1)} %copy-done.3, s32[3,768]{1,0:T(4,128)S(1)} %copy-done.4, f32[1,256]{1,0:T(1,128)S(1)} %bitcast.1), custom_call_target="tpu_custom_call" | custom-call | tf_op jit(solution)/shard_map/exchange/pallas_call | solution.py:174
  28.4 0.0 copy-done.1
  28.4 0.0 copy-done.2
  28.4 22.2 %tiles.1 = f32[1,1,7,20736]{3,2,1,0:T(8,128)S(1)} custom-call(f32[4,4,152,128]{3,2,1,0:T(8,128)S(1)} %exchange.1.got_ref, bf16[144,48]{1,0:T(8,128)(2,1)S(1)} %copy-done.2, s32[72,128]{1,0:T(8,128)S(1)} %copy-done.1), custom_call_target="tpu_custom_call" | custom-call | tf_op jit(solution)/shard_map/tiles/pallas_call | solution.py:334
  50.6 1.4 %copy.8 = f32[1,1,7,20736]{3,1,2,0:T(1,128)} copy(f32[1,1,7,20736]{3,2,1,0:T(8,128)S(1)} %tiles.1) | data formatting | bytes 1161216 | tf_op jit(solution)/shard_map/tiles/pallas_call | solution.py:334
Async XLA Ops:
  0.0 0.9 %copy-start = (f32[18,768]{1,0:T(8,128)S(1)}, f32[18,768]{1,0:T(8,128)}, u32[]{:S(2)}) copy-start(f32[18,768]{1,0:T(8,128)} %refs_1_.1) | copy-start | bytes 165892
  0.9 0.7 %copy-start.3 = (f32[6,768]{1,0:T(8,128)S(1)}, f32[6,768]{1,0:T(8,128)}, u32[]{:S(2)}) copy-start(f32[6,768]{1,0:T(8,128)} %refs_2_.1) | copy-start | bytes 55300
  1.6 0.7 %copy-start.4 = (s32[3,768]{1,0:T(4,128)S(1)}, s32[3,768]{1,0:T(4,128)}, u32[]{:S(2)}) copy-start(s32[3,768]{1,0:T(4,128)} %refs_3_.1) | copy-start | bytes 27652
  2.3 0.7 %copy-start.5 = (f32[2,768]{1,0:T(2,128)S(1)}, f32[2,768]{1,0:T(2,128)}, u32[]{:S(2)}) copy-start(f32[2,768]{1,0:T(2,128)} %refs_0_.1) | copy-start | bytes 18436
  3.0 0.7 %copy-start.6 = (f32[256]{0:T(256)S(1)}, f32[256]{0:T(256)}, u32[]{:S(2)}) copy-start(f32[256]{0:T(256)} %param.11) | copy-start | bytes 3076
  3.7 24.7 %copy-start.1 = (s32[72,128]{1,0:T(8,128)S(1)}, s32[72,128]{1,0:T(8,128)}, u32[]{:S(2)}) copy-start(s32[72,128]{1,0:T(8,128)} %constant.5.clone.group_ref) | copy-start | bytes 110596
  3.7 24.7 %copy-start.2 = (bf16[144,48]{1,0:T(8,128)(2,1)S(1)}, bf16[144,48]{1,0:T(8,128)(2,1)}, u32[]{:S(2)}) copy-start(bf16[144,48]{1,0:T(8,128)(2,1)} %constant.4.clone.repeat_ref) | copy-start | bytes 41476
where the time goes:
time: 52.3 us; the launch traced here: 52 us
  Pallas kernels  46.9 us (90%)
  local copies, waits for them, and re-layouts  5.11 us (10%)
    pallas_call x1, Pallas kernels, exchange(): pl.pallas_call(functools.partial(exchange_body, direct, n), out_shape=jax...  24.7 us
    pallas_call x1, Pallas kernels, tiles(): pl.pallas_call(functools.partial(tiles_body, n), out_shape=jax.ShapeDtype...  22.2 us
    unnamed x14, local copies, waits for them, and re-layouts  3.7 us
    pallas_call x1, local copies, waits for them, and re-layouts, tiles(): pl.pallas_call(functools.partial(tiles_body, n), out_shape=jax.ShapeDtype...  1.41 us

commit v1 on v0

v1 whole, which is shorter than its diff:
```python
import functools

import jax
import jax.numpy as jnp
from jax import lax
from jax.experimental import pallas as pl
from jax.experimental.pallas import tpu as pltpu
from jax.sharding import PartitionSpec as P

CAMERAS_PER_BLK = 16
TS = 144
HOPS = 3
OWNERS = HOPS + 1
TILES = 2 * HOPS + 1
KC = 3
TRACKS = 256
SLOTS = 12
LANES = 128
MSG = 152
DIRECT_DEVICES = 8
MESH = pl.DeviceIdType.MESH


def split(x):
    high = x.astype(jnp.bfloat16)
    low = (x - high.astype(jnp.float32)).astype(jnp.bfloat16)
    return high, low


def scaled_rows(residuals, camera_jac, point_jac, index):
    first, second = residuals[0:1], residuals[1:2]
    magnitude = jnp.sqrt(first * first + second * second)
    weight = index[2:3].astype(jnp.float32) / jnp.maximum(magnitude, 1.0)
    root = jnp.sqrt(weight)
    return (
        camera_jac * root,
        point_jac * root,
        index[1:2].astype(jnp.float32),
        index[0:1].astype(jnp.float32),
    )


def fused_body(direct, n, *refs):
    if direct:
        res_hbm, cam_hbm, pnt_hbm, idx_hbm, damp_hbm, out_ref = refs[:6]
        res_ref, cam_ref, pnt_ref, idx_ref, damp_ref = refs[6:11]
        rows_ref, send_ref, recv_ref, ssem1, rsem1 = refs[11:16]
        inputs = (
            (res_hbm, res_ref),
            (cam_hbm, cam_ref),
            (pnt_hbm, pnt_ref),
            (idx_hbm, idx_ref),
            (damp_hbm, damp_ref),
        )
        rest = refs[16:]
    else:
        rows_hbm, damp_hbm, out_ref, rows_ref, damp_ref = refs[:5]
        inputs = ((rows_hbm, rows_ref), (damp_hbm, damp_ref))
        rest = refs[5:]
    insem, ssem2, rsem2, ssem3, rsem3, got_ref, rep, coup, view, left, right, acc_a, acc_b = rest
    me = lax.axis_index("trk")
    col = lax.axis_index("cam")
    core = col + 1 - 2 * lax.rem(col, 2)
    side = lax.rem(col + 2, 4)

    def ahead(by):
        return lax.rem(me + by, n)

    loads = []
    for k, (src, dst) in enumerate(inputs):
        load = pltpu.make_async_copy(src, dst, insem.at[k])
        load.start()
        loads.append(load)
    barrier = pltpu.get_barrier_semaphore()
    steps = range(1, n) if direct else (1, 2, 3, n - 3, n - 2, n - 1)
    for by in steps:
        pl.semaphore_signal(barrier, inc=1, device_id=(ahead(by), col), device_id_type=MESH)
    for other in (core, side):
        pl.semaphore_signal(barrier, inc=1, device_id=(me, other), device_id_type=MESH)
    for load in loads:
        load.wait()

    if direct:
        width = rows_ref.shape[1] // n
        cj, pj, camera, position = scaled_rows(res_ref[...], cam_ref[...], pnt_ref[...], idx_ref[...])
        rows_ref[0:18] = cj
        rows_ref[18:24] = pj
        rows_ref[24:25] = camera
        rows_ref[25:26] = position
        rows_ref[26:32] = jnp.zeros((6, rows_ref.shape[1]), jnp.float32)
        rows = rows_ref[...]
        lane = lax.broadcasted_iota(jnp.int32, (32, LANES), 1)
        row = lax.broadcasted_iota(jnp.int32, (32, LANES), 0)
        fill = jnp.where(row == 25, -1.0, 0.0)
        for e in range(n):
            start = e * width
            piece = rows if start == 0 else pltpu.roll(rows, rows.shape[1] - start, 1)
            send_ref[e] = jnp.where(lane < width, piece[:, :LANES], fill)
    pl.semaphore_wait(barrier, len(steps) + 2)

    copies = []
    if direct:
        for by in range(1, n):
            copy = pltpu.make_async_remote_copy(
                src_ref=send_ref.at[ahead(by)],
                dst_ref=recv_ref.at[by],
                send_sem=ssem1.at[by],
                recv_sem=rsem1.at[by],
                device_id=(ahead(by), col),
                device_id_type=MESH,
            )
            copy.start()
            copies.append(copy)
        recv_ref[0] = send_ref[me]

    acc_a[...] = jnp.zeros_like(acc_a)
    acc_b[...] = jnp.zeros_like(acc_b)
    slot_row = lax.broadcasted_iota(jnp.int32, (72, LANES), 0)
    group = lax.shift_right_logical(slot_row * 57, 9)
    rep_row = lax.broadcasted_iota(jnp.int32, (TS, 48), 0)
    rep_col = lax.broadcasted_iota(jnp.int32, (TS, 48), 1)
    rep_col = jnp.where(rep_col < 24, rep_col, rep_col - 24)
    rep_row = jnp.where(rep_row < 72, rep_row, rep_row - 72)
    second_half = lax.broadcasted_iota(jnp.int32, (TS, 48), 0) >= 72
    parameter = rep_row - 9 * lax.shift_right_logical(rep_row * 57, 9)
    repeat = jnp.where(
        rep_col == jnp.where(second_half, parameter + 9, parameter), 1.0, 0.0
    ).astype(jnp.bfloat16)

    if direct:
        for copy in copies:
            copy.wait_recv()
        chunks = [recv_ref[k] for k in range(n)]
    else:
        chunks = [rows_ref[:, k * LANES : (k + 1) * LANES] for k in range(rows_ref.shape[1] // LANES)]
    slot = lax.broadcasted_iota(jnp.int32, (KC * TRACKS, LANES), 0).astype(jnp.float32)
    places, values = [], []
    for chunk in chunks:
        places.append(jnp.where(slot == chunk[25:26], 1.0, 0.0).astype(jnp.bfloat16))
        high, low = split(chunk)
        values.append(jnp.concatenate([high, low], axis=0))
    placed = lax.dot_general(
        jnp.concatenate(values, axis=1),
        jnp.concatenate(places, axis=1),
        (((1,), (1,)), ((), ())),
        preferred_element_type=jnp.float32,
    )
    placed = placed[:32] + placed[32:]
    tiles = KC * TRACKS // LANES
    for r in range(3):
        for l in range(tiles):
            at = (r * tiles + l) * 8
            got_ref[0, 0, at : at + 8] = placed[8 * r : 8 * r + 8, l * LANES : (l + 1) * LANES]
    for l in range(tiles):
        got_ref[0, 0, 144 + l : 145 + l] = placed[24:25, l * LANES : (l + 1) * LANES]
    for l in range(2):
        got_ref[0, 0, 150 + l : 151 + l] = damp_ref[:, l * LANES : (l + 1) * LANES]

    def message(src, dst, ssem, rsem, device):
        return pltpu.make_async_remote_copy(
            src_ref=src, dst_ref=dst, send_sem=ssem, recv_sem=rsem, device_id=device, device_id_type=MESH
        )

    def along(h):
        return message(got_ref.at[0, 0], got_ref.at[h, 0], ssem2.at[h], rsem2.at[h], (ahead(h), col))

    def to_core(h):
        return message(got_ref.at[h, 0], got_ref.at[h, 1], ssem3.at[h, 1], rsem3.at[h, 1], (me, core))

    def to_side(h):
        return message(got_ref.at[h, 0], got_ref.at[h, 2], ssem3.at[h, 2], rsem3.at[h, 2], (me, side))

    def passed(h):
        return message(got_ref.at[h, 2], got_ref.at[h, 3], ssem3.at[h, 3], rsem3.at[h, 3], (me, core))

    to_side(0).start()
    to_core(0).start()
    for h in range(1, OWNERS):
        along(h).start()
    to_side(0).wait_recv()
    passed(0).start()

    cameras = 2 * n * CAMERAS_PER_BLK
    left_parity = col // 2
    right_parity = lax.rem(col, 2)

    def per_slab(h, _):
        slab = lax.rem(me + n - h, n)
        to_core(h).wait_recv()
        passed(h).wait_recv()

        def per_part(part, sums):
            sums = list(sums)
            blocks = [
                jnp.concatenate(
                    [got_ref[h, part, (r * 6 + l) * 8 : (r * 6 + l) * 8 + 8] for r in range(3)], axis=0
                )
                for l in range(6)
            ]
            high, low = split(jnp.concatenate(blocks, axis=1))
            rep[...] = lax.dot_general(
                repeat,
                jnp.concatenate([high, low], axis=0),
                (((1,), (0,)), ((), ())),
                preferred_element_type=jnp.float32,
            )
            for l in range(6):
                half = l % 2
                where = part * 6 + l
                seen = got_ref[h, part, 144 + l : 145 + l].astype(jnp.int32) - 2 * CAMERAS_PER_BLK * slab
                view[where] = jnp.broadcast_to(jnp.where(seen < 0, seen + cameras, seen), (8, LANES))
                tile = blocks[l][16:24]
                first = [tile[2 + k : 3 + k] for k in range(3)]
                second = [tile[5 + k : 6 + k] for k in range(3)]
                one = rep[0:72, l * LANES : (l + 1) * LANES]
                two = rep[72:144, l * LANES : (l + 1) * LANES]
                for k in range(3):
                    coup[where, k] = one * first[k] + two * second[k]
                at = 6 * half
                for k, m in ((0, 0), (0, 1), (0, 2), (1, 1), (1, 2), (2, 2)):
                    sums[at] = sums[at] + first[k] * first[m] + second[k] * second[m]
                    at += 1
            return tuple(sums)

        sums = lax.fori_loop(0, 4, per_part, tuple(jnp.zeros((1, LANES), jnp.float32) for _ in range(12)))

        @pl.when(h < HOPS)
        def _():
            along(h + 1).wait_recv()
            to_side(h + 1).start()
            to_core(h + 1).start()

        inverse = []
        for half in range(2):
            a, b, c, d, e, f = sums[6 * half : 6 * half + 6]
            damp = got_ref[h, 0, 150 + half : 151 + half]
            a, d, f = a + damp, d + damp, f + damp
            cof = [d * f - e * e, c * e - b * f, b * e - c * d, a * f - c * c, b * c - a * e, a * d - b * b]
            det = a * cof[0] + b * cof[1] + c * cof[2]
            cof = [x / det for x in cof]
            inverse.append([[cof[i] for i in order] for order in ((0, 1, 2), (1, 3, 4), (2, 4, 5))])

        def gather(first_camera, half):
            halves = []
            for g in range(2):
                base = first_camera + 8 * g
                total = [None] * 3
                for s in range(SLOTS):
                    where = 2 * s + half
                    target = view[where] - base
                    mask = group == jnp.concatenate([target] * 9, axis=0)
                    for k in range(3):
                        term = jnp.where(mask, coup[where, k], 0.0)
                        total[k] = term if s == 0 else total[k] + term
                halves.append(total)
            return [jnp.concatenate([halves[0][k], halves[1][k]], axis=0) for k in range(3)]

        def store(ref, k, half, value):
            high, low = split(value)
            lanes = slice(k * TRACKS + half * LANES, k * TRACKS + (half + 1) * LANES)
            ref[0, :, lanes] = high
            ref[1, :, lanes] = low

        for half in range(2):
            panel = gather(CAMERAS_PER_BLK * (2 * h + left_parity), half)
            inv = inverse[half]
            for k in range(3):
                solved = panel[0] * inv[0][k] + panel[1] * inv[1][k] + panel[2] * inv[2][k]
                store(left, k, half, solved)

        for m in range(OWNERS):
            if m == 2:

                @pl.when(h < HOPS)
                def _():
                    to_side(h + 1).wait_recv()
                    passed(h + 1).start()

            for half in range(2):
                panel = gather(CAMERAS_PER_BLK * (2 * m + right_parity), half)
                for k in range(3):
                    store(right.at[m], k, half, panel[k])
            tile = lax.dot_general(
                jnp.concatenate([left[0], left[0], left[1]], axis=1),
                jnp.concatenate([right[m, 0], right[m, 1], right[m, 0]], axis=1),
                (((1,), (1,)), ((), ())),
                preferred_element_type=jnp.float32,
            )
            at = pl.multiple_of((HOPS - h + m) * TS, 8)
            acc_a[pl.ds(at, TS), :] += tile[:, :LANES]
            acc_b[pl.ds(at, TS), 0 : TS - LANES] += tile[:, LANES:]
        return 0

    lax.fori_loop(0, OWNERS, per_slab, 0)

    count = TILES * TS // 8
    lane = lax.broadcasted_iota(jnp.int32, (count, LANES), 1)
    main, tail = None, None
    for t in range(9):
        last_main, last_tail = main, tail
        if t < 8:
            rows = pl.ds(t, count, stride=8)
            main, tail = acc_a[rows, :], acc_b[rows, :]
            if t:
                main, tail = pltpu.roll(main, 16 * t, 1), pltpu.roll(tail, 16 * t, 1)
        if t == 0:
            value = main
        else:
            value = jnp.where(lane >= 16 * (t - 1), last_tail, last_main)
            if t < 8:
                value = jnp.where(lane >= 16 * t, main, value)
        out_ref[pl.ds(t, count, stride=9), :] = value

    for copy in copies:
        copy.wait_send()
    for h in range(OWNERS):
        if h:
            along(h).wait_send()
        to_core(h).wait_send()
        to_side(h).wait_send()
        passed(h).wait_send()


def fused(n, direct, damping, *arrays):
    arrays = arrays + (damping.reshape(1, TRACKS),)
    dma = pltpu.SemaphoreType.DMA
    f32 = jnp.float32
    scratch = [pltpu.VMEM(x.shape, x.dtype) for x in arrays]
    if direct:
        scratch += [
            pltpu.VMEM((32, arrays[0].shape[1]), f32),
            pltpu.VMEM((n, 32, LANES), f32),
            pltpu.VMEM((n, 32, LANES), f32),
            dma((n,)),
            dma((n,)),
        ]
    scratch += [dma((5,)), dma((OWNERS,)), dma((OWNERS,)), dma((OWNERS, 4)), dma((OWNERS, 4))]
    scratch += [
        pltpu.VMEM((OWNERS, 4, MSG, LANES), f32),
        pltpu.VMEM((TS, KC * TRACKS), f32),
        pltpu.VMEM((2 * SLOTS, 3, 72, LANES), f32),
        pltpu.VMEM((2 * SLOTS, 8, LANES), jnp.int32),
        pltpu.VMEM((2, TS, 3 * TRACKS), jnp.bfloat16),
        pltpu.VMEM((OWNERS, 2, TS, 3 * TRACKS), jnp.bfloat16),
        pltpu.VMEM((TILES * TS, LANES), f32),
        pltpu.VMEM((TILES * TS, LANES), f32),
    ]
    out = pl.pallas_call(
        functools.partial(fused_body, direct, n),
        out_shape=jax.ShapeDtypeStruct((TILES * TS * TS // LANES, LANES), f32),
        in_specs=[pl.BlockSpec(memory_space=pltpu.HBM)] * len(arrays),
        out_specs=pl.BlockSpec(memory_space=pltpu.VMEM),
        scratch_shapes=scratch,
        compiler_params=pltpu.CompilerParams(
            collective_id=0, has_side_effects=True, vmem_limit_bytes=64 * 2**20 - 2**15
        ),
        name="fused",
    )(*arrays)
    return out.reshape(1, 1, TILES, TS * TS)


def body(n, residuals, camera_jac, point_jac, obs_index, damping):
    if n <= DIRECT_DEVICES:
        return fused(n, True, damping, residuals, camera_jac, point_jac, obs_index)
    rows = jnp.concatenate(scaled_rows(residuals, camera_jac, point_jac, obs_index), axis=0)
    rows = lax.all_to_all(rows, "trk", split_axis=1, concat_axis=1, tiled=True)
    return fused(n, False, damping, jnp.pad(rows, ((0, 6), (0, 0))))


def solution(mesh):
    by_row = P(None, ("trk", "cam"))
    return jax.shard_map(
        functools.partial(body, mesh.shape["trk"]),
        mesh=mesh,
        in_specs=(by_row, by_row, by_row, by_row, P("trk")),
        out_specs=P("trk", "cam", None, None),
        check_vma=False,
    )
```

time: 52.3 us -> 43 us (0.82)
  Pallas kernels: 46.9 us -> 40.3 us
  local copies, waits for them, and re-layouts: 5.11 us -> 2.44 us
    pallas_call x2 -> x1, Pallas kernels: 46.9 us -> 40.3 us  [fused(): pl.pallas_call(functools.partial(fused_body, direct, n), out_shape=jax.Sh...]
    unnamed x14 -> x0, local copies, waits for them, and re-layouts: 3.7 us -> none
    reshape x0 -> x1, local copies, waits for them, and re-layouts: none -> 2.44 us  [fused(): return out.reshape(1, 1, TILES, TS * TS)]
    pallas_call x1 -> x0, local copies, waits for them, and re-layouts: 1.41 us -> none  [tiles(): pl.pallas_call(functools.partial(tiles_body, n), out_shape=jax.ShapeDtype...]
where the time goes in v1:
time: 43 us; the launch traced here: 42.8 us
  Pallas kernels  40.3 us (94%)
  local copies, waits for them, and re-layouts  2.44 us (6%)
    pallas_call x1, Pallas kernels, fused(): pl.pallas_call(functools.partial(fused_body, direct, n), out_shape=jax.Sh...  40.3 us
    reshape x1, local copies, waits for them, and re-layouts, fused(): return out.reshape(1, 1, TILES, TS * TS)  2.44 us

profile of v1, /device:TPU:0, one launch (start us, length us, event | category | flops | bytes accessed | tf_op | source)
XLA Modules:
  0.0 42.8 jit_solution(5583717784550203376)
XLA Ops:
  0.0 40.3 %fused.1 = f32[1134,128]{1,0:T(8,128)} custom-call(f32[2,768]{1,0:T(2,128)} %refs_0_.1, f32[18,768]{1,0:T(8,128)} %refs_1_.1, f32[6,768]{1,0:T(8,128)} %refs_2_.1, s32[3,768]{1,0:T(4,128)} %refs_3_.1, f32[1,256]{1,0:T(1,128)} %bitcast.1), custom_call_target="tpu_custom_call" | custom-call | tf_op jit(solution)/shard_map/fused/pallas_call | solution.py:348
  40.3 2.4 %reshape.8 = f32[1,1,7,20736]{3,1,2,0:T(1,128)} reshape(f32[1134,128]{1,0:T(8,128)} %fused.1) | data formatting | bytes 1161216 | tf_op jit(solution)/shard_map/reshape | solution.py:359

commit v2 on v1

--- a/solution.py
+++ b/solution.py
@@ -179,6 +179,9 @@
         along(h).start()
     to_side(0).wait_recv()
     passed(0).start()
+    along(1).wait_recv()
+    to_side(1).start()
+    to_core(1).start()
 
     cameras = 2 * n * CAMERAS_PER_BLK
     left_parity = col // 2
@@ -224,11 +227,11 @@
 
         sums = lax.fori_loop(0, 4, per_part, tuple(jnp.zeros((1, LANES), jnp.float32) for _ in range(12)))
 
-        @pl.when(h < HOPS)
+        @pl.when(h < HOPS - 1)
         def _():
-            along(h + 1).wait_recv()
-            to_side(h + 1).start()
-            to_core(h + 1).start()
+            along(h + 2).wait_recv()
+            to_side(h + 2).start()
+            to_core(h + 2).start()
 
         inverse = []
         for half in range(2):

time: 43 us -> 40.4 us (0.940)
  Pallas kernels: 40.3 us -> 37.7 us
    pallas_call x1, Pallas kernels: 40.3 us -> 37.7 us  [fused(): pl.pallas_call(functools.partial(fused_body, direct, n), out_shape=jax.Sh...]
where the time goes in v2:
time: 40.4 us; the launch traced here: 40.2 us
  Pallas kernels  37.7 us (93%)
  local copies, waits for them, and re-layouts  2.44 us (6%)
    pallas_call x1, Pallas kernels, fused(): pl.pallas_call(functools.partial(fused_body, direct, n), out_shape=jax.Sh...  37.7 us
    reshape x1, local copies, waits for them, and re-layouts, fused(): return out.reshape(1, 1, TILES, TS * TS)  2.44 us

profile of v2, /device:TPU:0, one launch (start us, length us, event | category | flops | bytes accessed | tf_op | source)
XLA Modules:
  0.0 40.2 jit_solution(2229155031547495078)
XLA Ops:
  0.0 37.7 %fused.1 = f32[1134,128]{1,0:T(8,128)} custom-call(f32[2,768]{1,0:T(2,128)} %refs_0_.1, f32[18,768]{1,0:T(8,128)} %refs_1_.1, f32[6,768]{1,0:T(8,128)} %refs_2_.1, s32[3,768]{1,0:T(4,128)} %refs_3_.1, f32[1,256]{1,0:T(1,128)} %bitcast.1), custom_call_target="tpu_custom_call" | custom-call | tf_op jit(solution)/shard_map/fused/pallas_call | solution.py:351
  37.7 2.4 %reshape.8 = f32[1,1,7,20736]{3,1,2,0:T(1,128)} reshape(f32[1134,128]{1,0:T(8,128)} %fused.1) | data formatting | bytes 1161216 | tf_op jit(solution)/shard_map/reshape | solution.py:362

commit v3 on v2

--- a/solution.py
+++ b/solution.py
@@ -272,7 +272,7 @@
                 store(left, k, half, solved)
 
         for m in range(OWNERS):
-            if m == 2:
+            if m == 1:
 
                 @pl.when(h < HOPS)
                 def _():

time: 40.4 us -> 41.3 us (1.022)
  Pallas kernels: 37.7 us -> 38.7 us
    pallas_call x1, Pallas kernels: 37.7 us -> 38.7 us  [fused(): pl.pallas_call(functools.partial(fused_body, direct, n), out_shape=jax.Sh...]
where the time goes in v3:
time: 41.3 us; the launch traced here: 41.1 us
  Pallas kernels  38.7 us (94%)
  local copies, waits for them, and re-layouts  2.44 us (6%)
    pallas_call x1, Pallas kernels, fused(): pl.pallas_call(functools.partial(fused_body, direct, n), out_shape=jax.Sh...  38.7 us
    reshape x1, local copies, waits for them, and re-layouts, fused(): return out.reshape(1, 1, TILES, TS * TS)  2.44 us

profile of v3, /device:TPU:0, one launch (start us, length us, event | category | flops | bytes accessed | tf_op | source)
XLA Modules:
  0.0 41.1 jit_solution(14978188448025703663)
XLA Ops:
  0.0 38.7 %fused.1 = f32[1134,128]{1,0:T(8,128)} custom-call(f32[2,768]{1,0:T(2,128)} %refs_0_.1, f32[18,768]{1,0:T(8,128)} %refs_1_.1, f32[6,768]{1,0:T(8,128)} %refs_2_.1, s32[3,768]{1,0:T(4,128)} %refs_3_.1, f32[1,256]{1,0:T(1,128)} %bitcast.1), custom_call_target="tpu_custom_call" | custom-call | tf_op jit(solution)/shard_map/fused/pallas_call | solution.py:351
  38.7 2.4 %reshape.8 = f32[1,1,7,20736]{3,1,2,0:T(1,128)} reshape(f32[1134,128]{1,0:T(8,128)} %fused.1) | data formatting | bytes 1161216 | tf_op jit(solution)/shard_map/reshape | solution.py:362
